TPU v7x, 32 devices: a whole 2x2x4 slice. The times are simulated.
32 devices in a mesh: groups: 2 (over y), hid: 4 (over x, core), mdl: 4 (over z).
Axes of the slice: x: 2, y: 2, z: 4, core: 2. Of those that a mesh axis runs over, the one named last changes fastest.
Arguments:
- tokens: bfloat16 [32, 2, 8192], P('groups', None, 'mdl'), parts along dimension 0, may hold values from -6 to 6
- norm_gain: bfloat16 [8192], P('mdl'), may hold values from 0.25 to 1.75
- query_weight: bfloat16 [8192, 8192], P('mdl', 'hid'), may hold values from -0.0625 to 0.0625
- key_weight: bfloat16 [8192, 1024], P('mdl', 'hid'), may hold values from -0.0625 to 0.0625
- value_weight: bfloat16 [8192, 1024], P('mdl', 'hid'), may hold values from -0.0625 to 0.0625
- query_bias: bfloat16 [8192], P('hid'), may hold values from -3 to 3
- key_bias: bfloat16 [1024], P('hid'), may hold values from -3 to 3
- value_bias: bfloat16 [1024], P('hid'), may hold values from -3 to 3
- out_weight: bfloat16 [8192, 8192], P('hid', 'mdl'), may hold values from -4 to 4
- key_cache: bfloat16 [32, 4096, 1024], P(('groups', 'hid'), 'mdl'), parts along dimension 0, may hold values from -500 to 500
- value_cache: bfloat16 [32, 4096, 1024], P(('groups', 'hid'), 'mdl'), parts along dimension 0, may hold values from -6 to 6
- lengths: int32 [32], P('groups'), parts along dimension 0, may hold values from 512 to 4096, as said below
Outputs:
- attention_out: bfloat16 [32, 2, 8192], P(('groups', 'hid'), None, 'mdl'), parts along dimension 0
There are 2 independent parts, one for each index of `groups`. A program takes and returns all parts, laid end to end along the dimension named above; an argument that names none is the same for every part. Nothing has to cross between parts.
Inputs may be any that keep to these rules, and one draw needn't show every extreme that they name: `lengths`: one row of each part holds 4096 keys and another 4096 / 8.
All inputs are finite; a program needn't handle non-finite values.
Results may differ from a plain program's by a relative error of at most 0.03.
Values may be sent and summed in bfloat16 or wider, within the bound.
A program may use at most 128 MiB of HBM per device.

v0:
```python
import math

import jax
import jax.numpy as jnp
from jax import lax
from jax.sharding import PartitionSpec as P

D = 8192
HEADS = 64
KV_HEADS = 8
HEAD_DIM = 128


epsilon = 1e-06
rope_base = 1000000.0


def combined_all(value, axis, combine):
    everything = jax.tree.map(
        lambda part, kind: lax.all_gather(part.astype(kind), axis),
        value,
        (jnp.bfloat16, jnp.bfloat16, jnp.bfloat16),
    )

    def take(k):
        return jax.tree.map(lambda part, own: part[k].astype(own.dtype), everything, value)

    return lax.fori_loop(
        1, lax.axis_size(axis), lambda k, so_far: combine(so_far, take(k)), take(0)
    )


def rotate_pairs(values, positions):
    half = values.shape[-1] // 2
    freq = rope_base ** (-jnp.arange(half, dtype=jnp.float32) * 2.0 / values.shape[-1])
    angles = positions.astype(jnp.float32)[..., None, None] * freq
    cosine = jnp.cos(angles)
    sine = jnp.sin(angles)
    lower = values[..., :half]
    upper = values[..., half:]
    return jnp.concatenate([lower * cosine - upper * sine, upper * cosine + lower * sine], axis=-1)


def join_parts(left_part, right_part):
    left_max, left_sum, left_acc = left_part
    right_max, right_sum, right_acc = right_part
    joined_max = jnp.maximum(left_max, right_max)
    left_factor = jnp.exp(left_max - joined_max)
    right_factor = jnp.exp(right_max - joined_max)
    joined_sum = left_sum * left_factor + right_sum * right_factor
    joined_acc = left_acc * left_factor[..., None] + right_acc * right_factor[..., None]
    return (joined_max, joined_sum, joined_acc)


def body(
    tokens,
    norm_gain,
    query_weight,
    key_weight,
    value_weight,
    query_bias,
    key_bias,
    value_bias,
    out_weight,
    key_cache,
    value_cache,
    lengths,
):
    row_count = tokens.shape[0]
    steps_count = tokens.shape[1]
    hid_count = lax.axis_size("hid")
    local_rows = key_cache.shape[0]
    local_len = key_cache.shape[1]
    group = HEADS // KV_HEADS
    query_width = query_weight.shape[1]
    key_width = key_weight.shape[1]
    proj_width = query_width + 2 * key_width
    inputs = tokens.astype(jnp.float32)
    square_sum = lax.psum(jnp.sum(inputs * inputs, axis=-1), "mdl")
    inv_rms = lax.rsqrt(square_sum / D + epsilon)
    row_scale = inv_rms.reshape(row_count * steps_count, 1)
    scaled = (
        (inputs * norm_gain.astype(jnp.float32))
        .astype(jnp.bfloat16)
        .reshape(row_count * steps_count, -1)
    )
    partial_value = jnp.concatenate(
        [
            jnp.dot(scaled, query_weight, preferred_element_type=jnp.float32),
            jnp.dot(scaled, key_weight, preferred_element_type=jnp.float32),
            jnp.dot(scaled, value_weight, preferred_element_type=jnp.float32),
        ],
        axis=1,
    )
    all_bias = jnp.concatenate([query_bias, key_bias, value_bias]).astype(jnp.float32)
    summed = lax.psum(partial_value.astype(jnp.bfloat16), "mdl").astype(jnp.float32)
    projected = (
        (summed * row_scale + all_bias)
        .astype(jnp.bfloat16)
        .reshape(row_count, steps_count, proj_width)
    )
    arrived = lax.all_to_all(projected, "hid", split_axis=0, concat_axis=2, tiled=True)
    blocks = arrived.reshape(local_rows, steps_count, hid_count, proj_width)
    query_lin = blocks[..., :query_width].reshape(local_rows, steps_count, HEADS, HEAD_DIM)
    key_lin = blocks[..., query_width : query_width + key_width].reshape(
        local_rows, steps_count, KV_HEADS, HEAD_DIM
    )
    value_new = blocks[..., query_width + key_width :].reshape(
        local_rows, steps_count, KV_HEADS, HEAD_DIM
    )
    my_lengths = lax.dynamic_slice_in_dim(
        lengths, lax.axis_index("hid") * local_rows, local_rows, 0
    )
    positions = my_lengths[:, None] + jnp.arange(steps_count, dtype=jnp.int32)[None, :]
    queries = rotate_pairs(query_lin.astype(jnp.float32), positions).astype(jnp.bfloat16)
    key_new = rotate_pairs(key_lin.astype(jnp.float32), positions).astype(jnp.bfloat16)
    grouped = queries.reshape(local_rows, steps_count, KV_HEADS, group, HEAD_DIM).transpose(
        0, 2, 1, 3, 4
    )
    grouped = grouped.reshape(local_rows, KV_HEADS, steps_count * group, HEAD_DIM)
    cache_keys = key_cache.reshape(local_rows, local_len, KV_HEADS, HEAD_DIM)
    cache_values = value_cache.reshape(local_rows, local_len, KV_HEADS, HEAD_DIM)
    score_scale = 1.0 / math.sqrt(HEAD_DIM)
    scores = (
        jnp.einsum("rkqd,rskd->rkqs", grouped, cache_keys, preferred_element_type=jnp.float32)
        * score_scale
    )
    cache_place = lax.axis_index("mdl") * local_len + jnp.arange(local_len, dtype=jnp.int32)
    visible = (cache_place[None, :] < my_lengths[:, None])[:, None, None, :]
    masked = jnp.where(visible, scores, -1e30)
    local_max = jnp.max(masked, axis=-1)
    weights = jnp.where(visible, jnp.exp(masked - local_max[..., None]), 0.0)
    local_sum = jnp.sum(weights, axis=-1)
    local_acc = jnp.einsum(
        "rkqs,rskd->rkqd",
        weights.astype(jnp.bfloat16),
        cache_values,
        preferred_element_type=jnp.float32,
    )
    run_max, run_sum, run_acc = combined_all((local_max, local_sum, local_acc), "mdl", join_parts)
    new_scores = (
        jnp.einsum("rkqd,rukd->rkqu", grouped, key_new, preferred_element_type=jnp.float32)
        * score_scale
    )
    query_step = jnp.arange(steps_count * group, dtype=jnp.int32) // group
    causal = (jnp.arange(steps_count, dtype=jnp.int32)[None, :] <= query_step[:, None])[None, None]
    new_masked = jnp.where(causal, new_scores, -1e30)
    new_max = jnp.maximum(run_max, jnp.max(new_masked, axis=-1))
    shrink = jnp.exp(run_max - new_max)
    new_weights = jnp.where(causal, jnp.exp(new_masked - new_max[..., None]), 0.0)
    total = run_sum * shrink + jnp.sum(new_weights, axis=-1)
    combined = run_acc * shrink[..., None] + jnp.einsum(
        "rkqu,rukd->rkqd",
        new_weights.astype(jnp.bfloat16),
        value_new,
        preferred_element_type=jnp.float32,
    )
    attended = combined / total[..., None]
    attended = attended.reshape(local_rows, KV_HEADS, steps_count, group, HEAD_DIM).transpose(
        0, 2, 1, 3, 4
    )
    attended = attended.reshape(local_rows, steps_count, HEADS * HEAD_DIM).astype(jnp.bfloat16)
    by_heads = lax.all_to_all(attended, "hid", split_axis=2, concat_axis=0, tiled=True)
    flat_heads = by_heads.reshape(row_count * steps_count, query_width)
    result = lax.psum_scatter(
        jnp.dot(flat_heads, out_weight, preferred_element_type=jnp.float32).astype(jnp.bfloat16),
        "hid",
        scatter_dimension=0,
        tiled=True,
    )
    return result.reshape(local_rows, steps_count, -1)


def solution(mesh):
    placed = (
        P("groups", None, "mdl"),
        P("mdl"),
        P("mdl", "hid"),
        P("mdl", "hid"),
        P("mdl", "hid"),
        P("hid"),
        P("hid"),
        P("hid"),
        P("hid", "mdl"),
        P(("groups", "hid"), "mdl", None),
        P(("groups", "hid"), "mdl", None),
        P("groups"),
    )
    return jax.shard_map(
        body,
        mesh=mesh,
        in_specs=placed,
        out_specs=P(("groups", "hid"), None, "mdl"),
        check_vma=False,
    )
```

profile of v0, /device:TPU:0, one launch (start us, length us, event | category | flops | bytes accessed | tf_op | source)
XLA Modules:
  0.0 191.8 jit_solution(4693880522193295256)
XLA Ops:
  6.5 0.0 copy-start
  6.5 0.0 all-reduce.2.cloned.1.call-start
  6.5 0.8 convert_element_type.154
  7.3 1.1 fusion.26
  8.5 0.1 reshape.196
  8.5 0.0 copy-done
  8.5 0.3 convolution_convert_fusion.2
  8.8 1.5 convolution_convert_fusion.3
  10.3 0.0 copy-start.4
  10.3 0.0 copy-start.1
  10.3 0.0 copy-start.2
  10.4 0.0 copy-start.3
  10.4 4.9 %convolution_convert_fusion.1 = bf16[32,2048]{1,0:T(8,128)(2,1)S(1)} fusion(bf16[32,2048]{1,0:T(8,128)(2,1)S(1)} %reshape.196, bf16[2048,2048]{1,0:T(8,128)(2,1)} %param.16), kind=kOutput, calls=%fused_computation.15 | convolution fusion | flops 268500992 | bytes 8650752 | tf_op jit(solution)/shard_map/dot_general | solution.py:89
  15.3 0.7 pad_maximum_fusion
  16.0 0.0 all-reduce.2.cloned.1.call-update
  16.0 0.0 copy-done.4
  16.0 0.1 dynamic_slice.33
  16.1 0.1 add_convert_fusion.3
  16.2 0.1 broadcast_compare_fusion
  16.3 13.7 %psum.15 = f32[16,2]{1,0:T(8,128)S(1)} all-reduce(f32[16,2]{1,0:T(8,128)S(1)} %get-tuple-element.210), channel_id=1, replica_groups=mesh['groups'=2,'hid'=4,'mdl'=4] {'mdl'}, use_global_device_ids=true, to_apply=%region_2.0 | all-reduce | flops 32 | bytes 256 | tf_op jit(solution)/shard_map/psum | solution.py:79
  30.0 0.1 multiply_cosine_fusion
  30.2 0.1 mul.214
  30.3 0.0 copy-done.1
  30.3 0.0 copy-done.2
  30.3 0.0 copy-done.3
  30.3 23.2 %all-reduce.2.cloned.1.call-done = bf16[32,2560]{1,0:T(8,128)(2,1)} async-done(((bf16[32,2560]{1,0:T(8,128)(2,1)}), bf16[32,2560]{1,0:T(8,128)(2,1)}) %all-reduce.2.cloned.1.call-update) | async-done | bytes 163856 | tf_op jit(solution)/shard_map/psum | solution.py:96
  53.5 1.0 add_convert_fusion
  54.5 0.7 reshape.197
  55.2 3.3 %all-to-all-start = ((bf16[16,2,2560]{2,1,0:T(2,128)(2,1)}), bf16[16,2,2560]{2,1,0:T(2,128)(2,1)S(1)}, u32[]{:S(2)}, u32[]{:S(2)}) async-start(bf16[16,2,2560]{2,1,0:T(2,128)(2,1)} %reshape.197), calls=%async_computation | async-start | bytes 327680 | tf_op jit(solution)/shard_map/all_to_all | solution.py:102
  58.6 0.0 reduce-scatter.2.cloned.1.call-start
  58.6 4.9 %all-to-all-done = bf16[16,2,2560]{2,1,0:T(2,128)(2,1)S(1)} async-done(((bf16[16,2,2560]{2,1,0:T(2,128)(2,1)}), bf16[16,2,2560]{2,1,0:T(2,128)(2,1)S(1)}, u32[]{:S(2)}, u32[]{:S(2)}) %all-to-all-start) | async-done | bytes 163872 | tf_op jit(solution)/shard_map/all_to_all | solution.py:102
  63.5 0.1 copy.105
  63.7 0.1 fusion.46
  63.8 0.1 reshape.207
  63.9 0.1 fusion.27
  64.1 5.8 %fusion.9 = (f32[4,8,16]{2,1,0:T(8,128)S(1)}, f32[4,8,16,1024]{3,2,1,0:T(8,128)S(1)}) fusion(pred[4,1024]{1,0:T(4,128)(4,1)S(1)} %broadcast_compare_fusion, bf16[4,1024,1024]{2,1,0:T(8,128)(2,1)} %param.23, bf16[4,2,8,8,64]{4,3,2,1,0:T(8,128)(2,1)S(1)} %get-tuple-element.207, bf16[4,2,8,8,64]{4,3,2,1,0:T(8,128)(2,1)S(1)} %get-tuple-element.206), kind=kOutput, calls=%fused_computation.18 | convolution fusion | flops 136052224 | bytes 10622976 | tf_op jit(solution)/shard_map/rkqd,rskd->rkqs/dot_general | solution.py:125
  69.9 0.7 fusion.11
  70.6 5.5 %fusion.14 = bf16[4,8,16,128]{3,2,1,0:T(8,128)(2,1)S(1)} fusion(f32[4,8,16,1024]{3,2,1,0:T(8,128)S(1)} %get-tuple-element.219, f32[4,8,16]{2,1,0:T(8,128)S(1)} %get-tuple-element.218, pred[4,1024]{1,0:T(4,128)(4,1)S(1)} %broadcast_compare_fusion, bf16[4,1024,1024]{2,1,0:T(8,128)(2,1)} %param.24), kind=kOutput, calls=%fused_computation.24 | convolution fusion | flops 136904704 | bytes 10622976 | tf_op jit(solution)/shard_map/rkqs,rskd->rkqd/dot_general | solution.py:134
  76.1 13.1 %all-gather = bf16[16,8,16]{2,1,0:T(8,128)(2,1)S(1)} all-gather(bf16[4,8,16]{2,1,0:T(8,128)(2,1)S(1)} %convert_element_type.162), channel_id=2, replica_groups=mesh['groups'=2,'hid'=4,'mdl'=4] {'mdl'}, dimensions={0}, use_global_device_ids=true | all-gather | bytes 5120 | tf_op jit(solution)/shard_map/all_gather | solution.py:20
  89.2 13.2 %all-gather.1 = bf16[16,8,16]{2,1,0:T(8,128)(2,1)S(1)} all-gather(bf16[4,8,16]{2,1,0:T(8,128)(2,1)S(1)} %fusion.11), channel_id=3, replica_groups=mesh['groups'=2,'hid'=4,'mdl'=4] {'mdl'}, dimensions={0}, use_global_device_ids=true | all-gather | bytes 5120 | tf_op jit(solution)/shard_map/all_gather | solution.py:20
  102.4 14.8 %all-gather.2 = bf16[16,8,16,128]{3,2,1,0:T(8,128)(2,1)S(1)} all-gather(bf16[4,8,16,128]{3,2,1,0:T(8,128)(2,1)S(1)} %fusion.14), channel_id=4, replica_groups=mesh['groups'=2,'hid'=4,'mdl'=4] {'mdl'}, dimensions={0}, use_global_device_ids=true | all-gather | bytes 655360 | tf_op jit(solution)/shard_map/all_gather | solution.py:20
  117.2 1.0 while.19
  117.2 0.3 fusion.61
  117.6 0.3 fusion.61
  117.9 0.3 fusion.61
  118.3 0.3 fusion.47
  118.5 0.1 fusion.38
  118.6 0.3 fusion.17
  118.9 4.9 %copy.68 = bf16[4,2,8,8,128]{0,1,4,3,2:T(2,128)(2,1)} copy(bf16[4,2,8,8,128]{4,3,1,2,0:T(8,128)(2,1)S(1)} %fusion.17) | data formatting | bytes 262144 | tf_op jit(solution)/shard_map/convert_element_type | solution.py:162
  123.8 8.7 %reshape.224 = bf16[4,2,8192]{2,1,0:T(2,128)(2,1)S(1)} reshape(bf16[8192,2,4]{2,1,0:T(2,128)(2,1)} %bitcast.78) | data formatting | bytes 262144
  132.5 7.0 %all_to_all.30 = bf16[4,2,8192]{2,1,0:T(2,128)(2,1)S(1)} all-to-all(bf16[4,2,8192]{2,1,0:T(2,128)(2,1)S(1)} %reshape.224), channel_id=1, replica_groups=mesh['groups'=2,'hid'=4,'mdl'=4] {'hid'}, dimensions={0} | all-to-all | bytes 262144 | tf_op jit(solution)/shard_map/all_to_all | solution.py:163
  139.5 10.0 %reshape.225 = bf16[8192,2,4]{2,1,0:T(2,128)(2,1)} reshape(bf16[4,2,8192]{2,1,0:T(2,128)(2,1)S(1)} %all_to_all.30) | data formatting | bytes 262144
  149.6 9.7 %copy.67 = bf16[4,2,4,2048]{3,1,0,2:T(2,128)(2,1)S(1)} copy(bf16[4,2,4,2048]{0,1,3,2:T(2,128)(2,1)} %bitcast.79) | data formatting | bytes 262144 | tf_op jit(solution)/shard_map/all_to_all | solution.py:163
  159.3 0.1 reshape.202
  159.3 5.6 %convolution_convert_fusion = bf16[32,2048]{1,0:T(8,128)(2,1)} fusion(bf16[32,2048]{1,0:T(8,128)(2,1)S(1)} %reshape.202, bf16[2048,2048]{1,0:T(8,128)(2,1)} %param.22), kind=kOutput, calls=%fused_computation.14 | convolution fusion | flops 268500992 | bytes 8650752 | tf_op jit(solution)/shard_map/dot_general | solution.py:166
  164.9 0.0 reduce-scatter.2.cloned.1.call-update
  164.9 18.6 %reduce-scatter.2.cloned.1.call-done = bf16[8,2048]{1,0:T(8,128)(2,1)} async-done(((bf16[32,2048]{1,0:T(8,128)(2,1)}), bf16[8,2048]{1,0:T(8,128)(2,1)}) %reduce-scatter.2.cloned.1.call-update) | async-done | bytes 32784 | tf_op jit(solution)/shard_map/reduce_scatter | solution.py:165
  183.6 1.4 reshape.203
  (20 shorter events, 0.3 us)
Async XLA Ops:
  6.5 2.0 %copy-start = (bf16[2048,256]{1,0:T(8,128)(2,1)S(1)}, bf16[2048,256]{1,0:T(8,128)(2,1)}, u32[]{:S(2)}) copy-start(bf16[2048,256]{1,0:T(8,128)(2,1)} %param.18) | copy-start | bytes 3145732
  6.5 47.0 %all-reduce.2.cloned.1.call-start = ((), (), s32[]{:S(2)}) async-start(), calls=%async_computation.3 | async-start | bytes 327680 | tf_op jit(solution)/shard_map/psum | solution.py:96
  10.3 5.7 %copy-start.4 = (s32[16]{0:T(128)S(1)}, s32[16]{0:T(128)}, u32[]{:S(2)}) copy-start(s32[16]{0:T(128)} %param.25) | copy-start | bytes 196
  10.3 19.9 %copy-start.1 = (bf16[2048]{0:T(1024)(128)(2,1)S(1)}, bf16[2048]{0:T(1024)(128)(2,1)}, u32[]{:S(2)}) copy-start(bf16[2048]{0:T(1024)(128)(2,1)} %param.19) | copy-start | bytes 12292
  10.3 19.9 %copy-start.2 = (bf16[256]{0:T(256)(128)(2,1)S(1)}, bf16[256]{0:T(256)(128)(2,1)}, u32[]{:S(2)}) copy-start(bf16[256]{0:T(256)(128)(2,1)} %param.21) | copy-start | bytes 1540
  10.4 19.9 %copy-start.3 = (bf16[256]{0:T(256)(128)(2,1)S(1)}, bf16[256]{0:T(256)(128)(2,1)}, u32[]{:S(2)}) copy-start(bf16[256]{0:T(256)(128)(2,1)} %param.20) | copy-start | bytes 1540
  55.2 8.3 %all-to-all-start = ((bf16[16,2,2560]{2,1,0:T(2,128)(2,1)}), bf16[16,2,2560]{2,1,0:T(2,128)(2,1)S(1)}, u32[]{:S(2)}, u32[]{:S(2)}) async-start(bf16[16,2,2560]{2,1,0:T(2,128)(2,1)} %reshape.197), calls=%async_computation | async-start | bytes 327680 | tf_op jit(solution)/shard_map/all_to_all | solution.py:102
  58.6 125.0 %reduce-scatter.2.cloned.1.call-start = ((), (), s32[]{:S(2)}) async-start(), calls=%async_computation.4 | async-start | bytes 163840 | tf_op jit(solution)/shard_map/reduce_scatter | solution.py:165
Sparse Core Ops, SparseCore 0:
  16.1 37.3 all-reduce.1
  165.1 18.4 reduce-scatter.1
where the time goes:
time: 193 us; the launch traced here: 192 us
  blocking collectives  61.8 us (32%)
  waiting for transfers between devices  46.7 us (24%)
  local copies, waits for them, and re-layouts  36 us (19%)
  matrix products  24.2 us (13%)
  between operations  13.7 us (7%)
  other arithmetic  5.87 us (3%)
  starting transfers between devices  3.39 us (2%)
    all_gather x3, blocking collectives, combined_all(): lax.all_gather(part.astype(kind), axis)  41.1 us
    psum x1, waiting for transfers between devices, body(): lax.psum(partial_value.astype(jnp.bfloat16), 'mdl').astype(jnp.float32)  23.2 us
    unnamed x12, local copies, waits for them, and re-layouts  18.7 us
    reduce_scatter x1, waiting for transfers between devices, body(): lax.psum_scatter(jnp.dot(flat_heads, out_weight, preferred_element_type=j...  18.6 us
    psum x1, blocking collectives, body(): square_sum = lax.psum(jnp.sum(inputs * inputs, axis=-1), 'mdl')  13.7 us
    all_to_all x1, local copies, waits for them, and re-layouts, body(): lax.all_to_all(attended, 'hid', split_axis=2, concat_axis=0, tiled=True)  9.69 us
    all_to_all x1, blocking collectives, body(): lax.all_to_all(attended, 'hid', split_axis=2, concat_axis=0, tiled=True)  7.02 us
    dot_general x1, matrix products, body(): jnp.einsum('rkqd,rskd->rkqs', grouped, cache_keys, preferred_element_type...  5.78 us
  transfers between devices with their start and end apart: 3, of which 3 were waited for; matrix products, arithmetic and copies ran while one was open for 0% of the time, Pallas kernels for 0%

commit v1 on v0

--- a/solution.py
+++ b/solution.py
@@ -2,7 +2,10 @@
 
 import jax
 import jax.numpy as jnp
+import numpy as np
 from jax import lax
+from jax.experimental import pallas as pl
+from jax.experimental.pallas import tpu as pltpu
 from jax.sharding import PartitionSpec as P
 
 D = 8192
@@ -170,6 +173,383 @@
     )
     return result.reshape(local_rows, steps_count, -1)
 
+def fused_kernel(
+    tokens_ref, gain_ref, bias_ref, freq_ref, lengths_ref, query_hbm, key_hbm, value_hbm, out_hbm, keys_hbm, values_hbm,
+    result_ref,
+    proj_w, out_w, keys, values,
+    send1, recv1, squares, recv_squares, send2, recv2, rotated, key_rot, value_rot, row_queries, row_keys, row_values,
+    send3, recv3, stats, recv_stats, send4, recv4, heads_f32, heads_in, partial_out, send5, recv5,
+    load_sem, s1, r1, sq_s, sq_r, s2, r2, s3, r3, st_s, st_r, s4, r4, s5, r5,
+):
+    hid_count, mdl_count = lax.axis_size("hid"), lax.axis_size("mdl")
+    me_h, me_m = lax.axis_index("hid"), lax.axis_index("mdl")
+    bf16, f32 = jnp.bfloat16, jnp.float32
+    rows = tokens_ref.shape[0]
+    own_rows = rows // hid_count
+    local_rows, local_len = keys.shape[0], keys.shape[1]
+    heads_out = proj_w.shape[2] // HEAD_DIM
+    query_width, key_width = query_hbm.shape[1], key_hbm.shape[1]
+    query_heads = query_width // HEAD_DIM
+    kv_local = key_width // HEAD_DIM
+    group = HEADS // KV_HEADS
+    block_rows = 2 * group
+    block_width = proj_w.shape[2]
+
+    def send(src, dst, send_sem, recv_sem, to):
+        return pltpu.make_async_remote_copy(
+            src_ref=src, dst_ref=dst, send_sem=send_sem, recv_sem=recv_sem,
+            device_id=to, device_id_type=pl.DeviceIdType.MESH,
+        )
+
+    loads = []
+
+    def load(src, dst):
+        copy = pltpu.make_async_copy(src, dst, load_sem.at[len(loads)])
+        copy.start()
+        loads.append(copy)
+        return copy
+
+    block_loads = []
+    parts = ((query_hbm, 0, query_width), (key_hbm, query_width, key_width), (value_hbm, query_width + key_width, key_width))
+    for b in range(mdl_count):
+        low, high = b * block_width, (b + 1) * block_width
+        mine = []
+        for ref, base, width in parts:
+            first, last = max(low, base), min(high, base + width)
+            if first < last:
+                mine.append(load(ref.at[:, first - base : last - base], proj_w.at[b, :, first - low : last - low]))
+        block_loads.append(mine)
+    keys_load = load(keys_hbm, keys)
+    values_load = load(values_hbm, values)
+    out_load = load(out_hbm, out_w)
+
+    others = [(dh, dm) for dh in range(hid_count) for dm in range(mdl_count) if dh or dm]
+
+    def partner(dh, dm):
+        return {"hid": lax.rem(me_h + dh, hid_count), "mdl": lax.rem(me_m + dm, mdl_count)}
+
+    barrier = pltpu.get_barrier_semaphore()
+    for dh, dm in others:
+        pl.semaphore_signal(barrier, inc=1, device_id=partner(dh, dm), device_id_type=pl.DeviceIdType.MESH)
+
+    inputs = tokens_ref[...].astype(f32)
+    square_col = jnp.sum(inputs * inputs, axis=-1, keepdims=True)
+    eye_in = (
+        lax.broadcasted_iota(jnp.int32, (rows, 128), 0) == lax.broadcasted_iota(jnp.int32, (rows, 128), 1)
+    )
+    square_row = jnp.sum(jnp.where(eye_in, square_col, 0.0), axis=0, keepdims=True)
+    squares[...] = jnp.broadcast_to(square_row, squares.shape)
+    scaled = (inputs * gain_ref[...].astype(f32)).astype(bf16)
+    pl.semaphore_wait(barrier, len(others))
+
+    square_copies = []
+    for d in range(1, mdl_count):
+        copy = send(squares, recv_squares.at[d], sq_s.at[d], sq_r.at[d], partner(0, d))
+        copy.start()
+        square_copies.append(copy)
+
+    def block_copy(d):
+        b = lax.rem(me_m + d, mdl_count)
+        return send(send1.at[b], recv1.at[d], s1.at[d], r1.at[d], {"mdl": b})
+
+    for b in range(mdl_count):
+        for copy in block_loads[b]:
+            copy.wait()
+        part = jnp.dot(scaled, proj_w[b], preferred_element_type=f32).astype(bf16)
+        for i in range(heads_out):
+            send1[b, i] = part[:, i * HEAD_DIM : (i + 1) * HEAD_DIM]
+
+        @pl.when(me_m != b)
+        def _():
+            block_copy(lax.rem(b - me_m + mdl_count, mdl_count)).start()
+
+    place = lax.broadcasted_iota(jnp.int32, (own_rows, HEAD_DIM), 0)
+    lane = lax.broadcasted_iota(jnp.int32, (own_rows, HEAD_DIM), 1)
+    position = place % 2
+    for r in range(local_rows):
+        position = position + jnp.where(place // 2 == r, lengths_ref[me_h * local_rows + r], 0)
+    half = HEAD_DIM // 2
+    angles = position.astype(f32) * freq_ref[...]
+    cosine = jnp.cos(angles)
+    sine = jnp.sin(angles)
+    sine = jnp.where(lane < half, -sine, sine)
+
+    for copy in square_copies:
+        copy.wait()
+    square_total = squares[...]
+    for d in range(1, mdl_count):
+        square_total = square_total + recv_squares[d]
+    square_sum = jnp.sum(jnp.where(eye_in, square_total[:1, :], 0.0), axis=1, keepdims=True)
+    inv_rms = lax.rsqrt(square_sum / D + epsilon)
+    for d in range(1, mdl_count):
+        block_copy(d).wait()
+    for i in range(heads_out):
+        total = send1[me_m, i].astype(f32)
+        for d in range(1, mdl_count):
+            total = total + recv1[d, i].astype(f32)
+        total = total * inv_rms + bias_ref[me_m, i]
+        for h in range(hid_count):
+            send2[h, i] = total[h * own_rows : (h + 1) * own_rows].astype(bf16)
+    recv2[me_h, me_m] = send2[me_h]
+    copies = []
+    for k, (dh, dm) in enumerate(others):
+        to = partner(dh, dm)
+        copy = send(send2.at[to["hid"]], recv2.at[me_h, me_m], s2.at[k], r2.at[k], to)
+        copy.start()
+        copies.append(copy)
+    for copy in copies:
+        copy.wait()
+
+    for h in range(hid_count):
+        x = recv2[h].astype(f32).reshape(mdl_count * heads_out, own_rows, HEAD_DIM)
+        turn = x[: query_heads + kv_local].reshape((query_heads + kv_local) * own_rows, HEAD_DIM)
+        turned = turn.reshape(-1, own_rows, HEAD_DIM) * cosine[None] + pltpu.roll(turn, half, 1).reshape(
+            -1, own_rows, HEAD_DIM
+        ) * sine[None]
+        n = query_heads * own_rows
+        rotated[h * n : (h + 1) * n] = turned[:query_heads].reshape(n, HEAD_DIM)
+        n = kv_local * own_rows
+        key_rot[h * n : (h + 1) * n] = turned[query_heads:].astype(bf16).astype(f32).reshape(n, HEAD_DIM)
+        value_rot[h * n : (h + 1) * n] = x[query_heads + kv_local :].reshape(n, HEAD_DIM)
+    for r in range(local_rows):
+        steps = [rotated[pl.ds(2 * r + t, HEADS, stride=own_rows), :] for t in range(2)]
+        for kv in range(KV_HEADS):
+            row_queries[r, kv] = jnp.concatenate(
+                [s[kv * group : (kv + 1) * group] for s in steps], axis=0
+            ).astype(bf16)
+        for t in range(2):
+            row_keys[r, t] = key_rot[pl.ds(2 * r + t, KV_HEADS, stride=own_rows), :]
+            row_values[r, t] = value_rot[pl.ds(2 * r + t, KV_HEADS, stride=own_rows), :]
+
+    keys_load.wait()
+    values_load.wait()
+    score_scale = 1.0 / math.sqrt(HEAD_DIM)
+    pair_rows = 2 * block_rows
+    columns = lax.broadcasted_iota(jnp.int32, (pair_rows, local_len), 1)
+    all_rows = KV_HEADS * block_rows
+    eye = (
+        lax.broadcasted_iota(jnp.int32, (all_rows, 128), 0) == lax.broadcasted_iota(jnp.int32, (all_rows, 128), 1)
+    )
+
+    def to_row(col):
+        return jnp.sum(jnp.where(eye, col, 0.0), axis=0, keepdims=True)
+
+    def to_col(row):
+        return jnp.sum(jnp.where(eye, row, 0.0), axis=1, keepdims=True)
+
+    def part_copy(d):
+        to = {"mdl": lax.rem(me_m + d, mdl_count)}
+        return send(send3.at[d], recv3.at[d], s3.at[d], r3.at[d], to)
+
+    def stat_copy(d):
+        to = {"mdl": lax.rem(me_m + d, mdl_count)}
+        return send(stats.at[d], recv_stats.at[d], st_s.at[d], st_r.at[d], to)
+
+    def one_row(step, carry):
+        d = lax.rem(step, mdl_count)
+        r = lax.rem(me_m + d, mdl_count)
+        visible = columns < lengths_ref[me_h * local_rows + r] - me_m * local_len
+        tops, sums = [], []
+        for p in range(KV_HEADS // 2):
+            qa, qb = row_queries[r, 2 * p], row_queries[r, 2 * p + 1]
+            none = jnp.zeros_like(qa)
+            left = jnp.concatenate(
+                [jnp.concatenate([qa, none], axis=1), jnp.concatenate([none, qb], axis=1)], axis=0
+            )
+            wide = slice(p * 2 * HEAD_DIM, (p + 1) * 2 * HEAD_DIM)
+            scores = lax.dot_general(
+                left, keys[r, :, wide], (((1,), (1,)), ((), ())), preferred_element_type=f32
+            ) * score_scale
+            masked = jnp.where(visible, scores, -1e30)
+            top = jnp.max(masked, axis=-1, keepdims=True)
+            weights = jnp.where(visible, jnp.exp(masked - top), 0.0)
+            tops.append(top)
+            sums.append(jnp.sum(weights, axis=-1, keepdims=True))
+            acc = jnp.dot(weights.astype(bf16), values[r, :, wide], preferred_element_type=f32)
+            send3[d, 2 * p] = acc[:block_rows, :HEAD_DIM].astype(bf16)
+            send3[d, 2 * p + 1] = acc[block_rows:, HEAD_DIM:].astype(bf16)
+        stats[d, 0] = jnp.broadcast_to(to_row(jnp.concatenate(tops, axis=0)), (8, 128))
+        stats[d, 1] = jnp.broadcast_to(to_row(jnp.concatenate(sums, axis=0)), (8, 128))
+
+        @pl.when(d != 0)
+        def _():
+            part_copy(d).start()
+            stat_copy(d).start()
+
+        return carry
+
+    lax.fori_loop(1, mdl_count + 1, one_row, 0)
+
+    query_all = row_queries[me_m].reshape(all_rows, HEAD_DIM).astype(f32)
+
+    def spread(rows8):
+        return jnp.concatenate(
+            [jnp.broadcast_to(rows8[kv : kv + 1], (block_rows, HEAD_DIM)) for kv in range(KV_HEADS)], axis=0
+        )
+
+    second = lax.broadcasted_iota(jnp.int32, (all_rows, 1), 0) % block_rows >= group
+    first_score = jnp.sum(query_all * spread(row_keys[me_m, 0]), axis=-1, keepdims=True) * score_scale
+    next_score = jnp.sum(query_all * spread(row_keys[me_m, 1]), axis=-1, keepdims=True) * score_scale
+    top = jnp.maximum(first_score, jnp.where(second, next_score, -1e30))
+    for d in range(1, mdl_count):
+        stat_copy(d).wait()
+        part_copy(d).wait()
+    held = [stats[0]] + [recv_stats[d] for d in range(1, mdl_count)]
+    part_tops = [to_col(s[0, :1]) for s in held]
+    part_sums = [to_col(s[1, :1]) for s in held]
+    for part_top in part_tops:
+        top = jnp.maximum(top, part_top)
+    first_weight = jnp.exp(first_score - top)
+    next_weight = jnp.where(second, jnp.exp(jnp.where(second, next_score, -1e30) - top), 0.0)
+    total = first_weight + next_weight
+    combined = first_weight.astype(bf16).astype(f32) * spread(row_values[me_m, 0]) + next_weight.astype(bf16).astype(
+        f32
+    ) * spread(row_values[me_m, 1])
+    for d in range(mdl_count):
+        factor = jnp.exp(part_tops[d] - top)
+        acc = send3[0] if d == 0 else recv3[d]
+        total = total + part_sums[d] * factor
+        combined = combined + acc.reshape(all_rows, HEAD_DIM).astype(f32) * factor
+    attended = (combined / total).astype(bf16)
+    send4[...] = attended.reshape(send4.shape)
+    recv4[me_h, me_m] = send4[me_h]
+    copies = []
+    for k, (dh, dm) in enumerate(others):
+        to = partner(dh, dm)
+        copy = send(send4.at[to["hid"]], recv4.at[me_h, me_m], s4.at[k], r4.at[k], to)
+        copy.start()
+        copies.append(copy)
+    for copy in copies:
+        copy.wait()
+    heads_f32[...] = recv4[...].astype(f32).reshape(heads_f32.shape)
+    senders = hid_count * mdl_count
+    for j in range(query_heads):
+        kv, g = j // group, j % group
+        both = [
+            heads_f32[pl.ds(kv * block_rows + t * group + g, senders, stride=pair_rows), :] for t in range(2)
+        ]
+        heads_in[:, j * HEAD_DIM : (j + 1) * HEAD_DIM] = jnp.concatenate(both, axis=0).astype(bf16)
+    out_load.wait()
+    partial_out[...] = jnp.dot(heads_in[...], out_w[...], preferred_element_type=f32)
+    for h in range(hid_count):
+        low = h * mdl_count
+        send5[h] = jnp.concatenate(
+            [partial_out[low : low + mdl_count], partial_out[senders + low : senders + low + mdl_count]], axis=0
+        ).astype(bf16)
+    copies = []
+    for d in range(1, hid_count):
+        to = lax.rem(me_h + d, hid_count)
+        copy = send(send5.at[to], recv5.at[d], s5.at[d], r5.at[d], {"hid": to})
+        copy.start()
+        copies.append(copy)
+    for copy in copies:
+        copy.wait()
+    summed = send5[me_h].astype(f32)
+    for d in range(1, hid_count):
+        summed = summed + recv5[d].astype(f32)
+    result_ref[...] = summed.astype(bf16)
+
+
+def fused_body(
+    tokens,
+    norm_gain,
+    query_weight,
+    key_weight,
+    value_weight,
+    query_bias,
+    key_bias,
+    value_bias,
+    out_weight,
+    key_cache,
+    value_cache,
+    lengths,
+):
+    row_count, steps_count, width = tokens.shape
+    hid_count, mdl_count = lax.axis_size("hid"), lax.axis_size("mdl")
+    local_rows, local_len = key_cache.shape[:2]
+    rows = row_count * steps_count
+    own_rows = rows // hid_count
+    proj_width = query_weight.shape[1] + 2 * key_weight.shape[1]
+    block_width = proj_width // mdl_count
+    heads_out = block_width // HEAD_DIM
+    group = HEADS // KV_HEADS
+    block_rows = steps_count * group
+    kv_local = KV_HEADS // hid_count
+    out_width = out_weight.shape[1]
+    others = hid_count * mdl_count - 1
+    bias = jnp.concatenate([query_bias, key_bias, value_bias]).astype(jnp.float32)
+    bias = bias.reshape(mdl_count, heads_out, 1, HEAD_DIM)
+    half = HEAD_DIM // 2
+    freq = jnp.asarray((rope_base ** (-2.0 * (np.arange(HEAD_DIM) % half) / HEAD_DIM)).astype(np.float32)[None])
+    bf16, f32 = jnp.bfloat16, jnp.float32
+    vmem, hbm = pl.BlockSpec(memory_space=pltpu.VMEM), pl.BlockSpec(memory_space=pl.ANY)
+    dma = pltpu.SemaphoreType.DMA
+    result = pl.pallas_call(
+        fused_kernel,
+        out_shape=jax.ShapeDtypeStruct((own_rows, out_width), bf16),
+        in_specs=[vmem, vmem, vmem, vmem, pl.BlockSpec(memory_space=pltpu.SMEM)] + [hbm] * 6,
+        out_specs=vmem,
+        scratch_shapes=[
+            pltpu.VMEM((mdl_count, width, block_width), bf16),
+            pltpu.VMEM(out_weight.shape, bf16),
+            pltpu.VMEM(key_cache.shape, bf16),
+            pltpu.VMEM(value_cache.shape, bf16),
+            pltpu.VMEM((mdl_count, heads_out, rows, HEAD_DIM), bf16),
+            pltpu.VMEM((mdl_count, heads_out, rows, HEAD_DIM), bf16),
+            pltpu.VMEM((8, 128), f32),
+            pltpu.VMEM((mdl_count, 8, 128), f32),
+            pltpu.VMEM((hid_count, heads_out, own_rows, HEAD_DIM), bf16),
+            pltpu.VMEM((hid_count, mdl_count, heads_out, own_rows, HEAD_DIM), bf16),
+            pltpu.VMEM((HEADS * own_rows, HEAD_DIM), f32),
+            pltpu.VMEM((KV_HEADS * own_rows, HEAD_DIM), f32),
+            pltpu.VMEM((KV_HEADS * own_rows, HEAD_DIM), f32),
+            pltpu.VMEM((local_rows, KV_HEADS, block_rows, HEAD_DIM), bf16),
+            pltpu.VMEM((local_rows, steps_count, KV_HEADS, HEAD_DIM), f32),
+            pltpu.VMEM((local_rows, steps_count, KV_HEADS, HEAD_DIM), f32),
+            pltpu.VMEM((mdl_count, KV_HEADS, block_rows, HEAD_DIM), bf16),
+            pltpu.VMEM((mdl_count, KV_HEADS, block_rows, HEAD_DIM), bf16),
+            pltpu.VMEM((mdl_count, 2, 8, 128), f32),
+            pltpu.VMEM((mdl_count, 2, 8, 128), f32),
+            pltpu.VMEM((hid_count, kv_local * block_rows, HEAD_DIM), bf16),
+            pltpu.VMEM((hid_count, mdl_count, kv_local * block_rows, HEAD_DIM), bf16),
+            pltpu.VMEM((hid_count * mdl_count * kv_local * block_rows, HEAD_DIM), f32),
+            pltpu.VMEM((rows, out_weight.shape[0]), bf16),
+            pltpu.VMEM((rows, out_width), f32),
+            pltpu.VMEM((hid_count, own_rows, out_width), bf16),
+            pltpu.VMEM((hid_count, own_rows, out_width), bf16),
+            dma((mdl_count + 5,)),
+            dma((mdl_count,)), dma((mdl_count,)),
+            dma((mdl_count,)), dma((mdl_count,)),
+            dma((others,)), dma((others,)),
+            dma((mdl_count,)), dma((mdl_count,)),
+            dma((mdl_count,)), dma((mdl_count,)),
+            dma((others,)), dma((others,)),
+            dma((hid_count,)), dma((hid_count,)),
+        ],
+        compiler_params=pltpu.CompilerParams(
+            collective_id=0, has_side_effects=True, vmem_limit_bytes=52 * 2**20
+        ),
+    )(
+        tokens.reshape(rows, width), norm_gain.reshape(1, width), bias, freq, lengths,
+        query_weight, key_weight, value_weight, out_weight, key_cache, value_cache,
+    )
+    return result.reshape(steps_count, local_rows, out_width).transpose(1, 0, 2)
+
+
+def choose(*arrays):
+    tokens, query_weight, key_weight, key_cache = arrays[0], arrays[2], arrays[3], arrays[9]
+    hid_count, mdl_count = lax.axis_size("hid"), lax.axis_size("mdl")
+    proj_width = query_weight.shape[1] + 2 * key_weight.shape[1]
+    fits = (
+        tokens.shape[1] == 2
+        and key_cache.shape[0] == mdl_count
+        and key_weight.shape[1] == 2 * HEAD_DIM
+        and KV_HEADS == 2 * hid_count
+        and proj_width % (mdl_count * HEAD_DIM) == 0
+        and tokens.shape[0] * 2 <= 128
+    )
+    return (fused_body if fits else body)(*arrays)
+
 
 def solution(mesh):
     placed = (
@@ -187,7 +567,7 @@
         P("groups"),
     )
     return jax.shard_map(
-        body,
+        choose,
         mesh=mesh,
         in_specs=placed,
         out_specs=P(("groups", "hid"), None, "mdl"),

time: 193 us -> 44.4 us (0.23)
  blocking collectives: 61.8 us -> 0 us
  waiting for transfers between devices: 46.7 us -> 0 us
  Pallas kernels: 0 us -> 38.6 us
  local copies, waits for them, and re-layouts: 36 us -> 4.86 us
  matrix products: 24.2 us -> 0 us
  between operations: 13.7 us -> 0.03 us
  other arithmetic: 5.87 us -> 0.73 us
  starting transfers between devices: 3.39 us -> 0 us
    all_gather x3 -> x0, blocking collectives: 41.1 us -> none  [combined_all(): lax.all_gather(part.astype(kind), axis)]
    pallas_call x0 -> x1, Pallas kernels: none -> 38.6 us  [fused_body(): pl.pallas_call(fused_kernel, out_shape=jax.ShapeDtypeStruct((own_rows, ou...]
    dot_general x8 -> x0, matrix products: 24.2 us -> none  [the longest x1 5.78 us: body(): jnp.einsum('rkqd,rskd->rkqs', grouped, cache_keys, preferred_element_type...]
    psum x1 -> x0, waiting for transfers between devices: 23.2 us -> none  [body(): lax.psum(partial_value.astype(jnp.bfloat16), 'mdl').astype(jnp.float32)]
    reduce_scatter x1 -> x0, waiting for transfers between devices: 18.6 us -> none  [body(): lax.psum_scatter(jnp.dot(flat_heads, out_weight, preferred_element_type=j...]
    unnamed x12 -> x6, local copies, waits for them, and re-layouts: 18.7 us -> 2.53 us
    psum x1 -> x0, blocking collectives: 13.7 us -> none  [body(): square_sum = lax.psum(jnp.sum(inputs * inputs, axis=-1), 'mdl')]
    all_to_all x2 -> x0, local copies, waits for them, and re-layouts: 9.78 us -> none  [the longest x1 9.69 us: body(): lax.all_to_all(attended, 'hid', split_axis=2, concat_axis=0, tiled=True)]
  transfers between devices with their start and end apart: 3 -> 0, of which waited for: 3 -> 0; matrix products, arithmetic and copies ran while one was open for 0% -> 0% of each run, Pallas kernels for 0% -> 0%
where the time goes in v1:
time: 44.4 us; the launch traced here: 44.2 us
  Pallas kernels  38.6 us (87%)
  local copies, waits for them, and re-layouts  4.86 us (11%)
  other arithmetic  0.73 us (2%)
    pallas_call x1, Pallas kernels, fused_body(): pl.pallas_call(fused_kernel, out_shape=jax.ShapeDtypeStruct((own_rows, ou...  38.6 us
    unnamed x6, local copies, waits for them, and re-layouts  2.53 us
    reshape x1, local copies, waits for them, and re-layouts, fused_body(): tokens.reshape(rows, width)  0.96 us

profile of v1, /device:TPU:0, one launch (start us, length us, event | category | flops | bytes accessed | tf_op | source)
XLA Modules:
  0.0 44.2 jit_solution(5878487564221010543)
XLA Ops:
  0.0 0.7 %reshape.23.gain_ref = bf16[1,2048]{1,0:T(2,128)(2,1)S(1)} reshape(bf16[2048]{0:T(1024)(128)(2,1)} %param.14) | data formatting | bytes 8192 | tf_op jit(solution)/shard_map/reshape | solution.py:533
  0.7 0.7 %maximum_convert_fusion = f32[2560]{0:T(1024)S(1)} fusion(bf16[256]{0:T(256)(128)(2,1)} %param.20, bf16[256]{0:T(256)(128)(2,1)} %param.19, bf16[2048]{0:T(1024)(128)(2,1)} %param.18), kind=kLoop, calls=%fused_computation.1 | loop fusion | flops 15360 | bytes 15360 | tf_op jit(solution)/shard_map/convert_element_type | solution.py:480
  1.4 1.0 %reshape.22.tokens_ref = bf16[32,2048]{1,0:T(8,128)(2,1)S(1)} reshape(bf16[16,2,2048]{2,1,0:T(2,128)(2,1)} %param.13) | data formatting | bytes 262144 | tf_op jit(solution)/shard_map/reshape | solution.py:533
  2.4 0.0 copy-start
  2.4 1.2 %copy-done = bf16[2048,256]{1,0:T(8,128)(2,1)S(1)} copy-done((bf16[2048,256]{1,0:T(8,128)(2,1)S(1)}, bf16[2048,256]{1,0:T(8,128)(2,1)}, u32[]{:S(2)}) %copy-start) | copy-done | bytes 1048600
  3.6 0.0 copy-start.1
  3.6 0.7 %copy-done.1 = s32[16]{0:T(128)S(1)} copy-done((s32[16]{0:T(128)S(1)}, s32[16]{0:T(128)}, u32[]{:S(2)}) %copy-start.1) | copy-done | bytes 88
  4.3 0.0 copy-start.2
  4.3 0.7 %copy-done.2 = f32[1,128]{1,0:T(1,128)S(1)} copy-done((f32[1,128]{1,0:T(1,128)S(1)}, f32[1,128]{1,0:T(1,128)}, u32[]{:S(2)}) %copy-start.2) | copy-done | bytes 536
  4.9 38.6 %shard_map.127 = bf16[8,2048]{1,0:T(8,128)(2,1)S(1)} custom-call(bf16[32,2048]{1,0:T(8,128)(2,1)S(1)} %reshape.22.tokens_ref, bf16[1,2048]{1,0:T(2,128)(2,1)S(1)} %reshape.23.gain_ref, f32[4,5,1,128]{3,2,1,0:T(1,128)S(1)} %reshape.25.bias_ref, f32[1,128]{1,0:T(1,128)S(1)} %copy-done.2, s32[16]{0:T(128)S(1)} %copy-done.1, bf16[2048,2048]{1,0:T(8,128)(2,1)} %query_hbm.1, ...), custom_call_target="tpu_custom_call" | custom-call | tf_op jit(solution)/shard_map/pallas_call | solution.py:487
  43.5 0.6 %copy.16 = bf16[2,4,2048]{2,0,1:T(2,128)(2,1)} copy(bf16[2,4,2048]{2,1,0:T(4,128)(2,1)S(1)} %reshape.24) | data formatting | bytes 65536 | tf_op jit(solution)/shard_map/reshape | solution.py:536
  (2 shorter events, 0.0 us)
Async XLA Ops:
  2.4 1.2 %copy-start = (bf16[2048,256]{1,0:T(8,128)(2,1)S(1)}, bf16[2048,256]{1,0:T(8,128)(2,1)}, u32[]{:S(2)}) copy-start(bf16[2048,256]{1,0:T(8,128)(2,1)} %key_hbm.1) | copy-start | bytes 3145732
  3.6 0.7 %copy-start.1 = (s32[16]{0:T(128)S(1)}, s32[16]{0:T(128)}, u32[]{:S(2)}) copy-start(s32[16]{0:T(128)} %lengths_ref.1) | copy-start | bytes 196
  4.3 0.7 %copy-start.2 = (f32[1,128]{1,0:T(1,128)S(1)}, f32[1,128]{1,0:T(1,128)}, u32[]{:S(2)}) copy-start(f32[1,128]{1,0:T(1,128)} %constant.2.clone.freq_ref) | copy-start | bytes 1540

commit v2 on v0

--- a/solution.py
+++ b/solution.py
@@ -2,7 +2,10 @@
 
 import jax
 import jax.numpy as jnp
+import numpy as np
 from jax import lax
+from jax.experimental import pallas as pl
+from jax.experimental.pallas import tpu as pltpu
 from jax.sharding import PartitionSpec as P
 
 D = 8192
@@ -170,6 +173,418 @@
     )
     return result.reshape(local_rows, steps_count, -1)
 
+def fused_kernel(
+    tokens_hbm, gain_hbm, query_bias_hbm, key_bias_hbm, value_bias_hbm, freq_hbm, lengths_ref,
+    query_hbm, key_hbm, value_hbm, out_hbm, keys_hbm, values_hbm,
+    result_ref,
+    tokens_in, gain_in, query_bias, key_bias, value_bias, freq_in, bias,
+    proj_w, out_w, keys, values,
+    send1, recv1, squares, recv_squares, send2, recv2, rotated, key_rot, value_rot, row_queries,
+    send3, recv3, stats, recv_stats, send4, recv4, heads_f32, heads_in, send5, recv5,
+    load_sem, block_sem, s1, r1, sq_s, sq_r, s2, r2, s3, r3, st_s, st_r, s4, r4, s5, r5,
+):
+    hid_count, mdl_count = lax.axis_size("hid"), lax.axis_size("mdl")
+    me_h, me_m = lax.axis_index("hid"), lax.axis_index("mdl")
+    bf16, f32 = jnp.bfloat16, jnp.float32
+    rows = tokens_in.shape[0] * tokens_in.shape[1]
+    own_rows = rows // hid_count
+    local_rows, local_len = keys.shape[0], keys.shape[1]
+    block_width = proj_w.shape[2]
+    heads_out = block_width // HEAD_DIM
+    query_width, key_width = query_hbm.shape[1], key_hbm.shape[1]
+    query_heads = query_width // HEAD_DIM
+    kv_local = key_width // HEAD_DIM
+    group = HEADS // KV_HEADS
+    block_rows = 2 * group
+    pair_rows = 2 * block_rows
+    far_first = (2, 3, 1, 0)
+
+    def other(me, d):
+        if d == 0:
+            return me
+        if d == 1:
+            return me + 1 - 2 * lax.rem(me, 2)
+        if d == 2:
+            return lax.rem(me + 2, 4)
+        return 3 - me
+
+    def send(src, dst, send_sem, recv_sem, to):
+        return pltpu.make_async_remote_copy(
+            src_ref=src, dst_ref=dst, send_sem=send_sem, recv_sem=recv_sem,
+            device_id=to, device_id_type=pl.DeviceIdType.MESH,
+        )
+
+    def partner(dh, dm):
+        return {"hid": other(me_h, dh), "mdl": other(me_m, dm)}
+
+    others = [(dh, dm) for dh in range(hid_count) for dm in far_first if dh or dm]
+    barrier = pltpu.get_barrier_semaphore()
+    for dh, dm in others:
+        pl.semaphore_signal(barrier, inc=1, device_id=partner(dh, dm), device_id_type=pl.DeviceIdType.MESH)
+
+    loads = []
+
+    def load(src, dst):
+        copy = pltpu.make_async_copy(src, dst, load_sem.at[len(loads)])
+        copy.start()
+        loads.append(copy)
+        return copy
+
+    small = [
+        load(tokens_hbm, tokens_in), load(gain_hbm, gain_in), load(query_bias_hbm, query_bias),
+        load(key_bias_hbm, key_bias), load(value_bias_hbm, value_bias), load(freq_hbm, freq_in),
+    ]
+    last = mdl_count - 1
+    tail = query_width - last * block_width
+    for d in far_first:
+        b = other(me_m, d)
+
+        @pl.when(b < last)
+        def _(b=b):
+            columns = pl.ds(pl.multiple_of(b * block_width, 128), block_width)
+            pltpu.make_async_copy(query_hbm.at[:, columns], proj_w.at[b], block_sem.at[b]).start()
+
+        @pl.when(b == last)
+        def _():
+            dst, sem = proj_w.at[last], block_sem.at[last]
+            pltpu.make_async_copy(query_hbm.at[:, last * block_width : query_width], dst.at[:, :tail], sem).start()
+            pltpu.make_async_copy(key_hbm, dst.at[:, tail : tail + key_width], sem).start()
+            pltpu.make_async_copy(value_hbm, dst.at[:, tail + key_width : block_width], sem).start()
+
+    keys_load = load(keys_hbm, keys)
+    values_load = load(values_hbm, values)
+    out_load = load(out_hbm, out_w)
+    for copy in small:
+        copy.wait()
+
+    inputs = tokens_in[...].astype(f32).reshape(rows, -1)
+    square_col = jnp.sum(inputs * inputs, axis=-1, keepdims=True)
+    eye_row = lax.broadcasted_iota(jnp.int32, (rows, 128), 0)
+    eye_lane = lax.broadcasted_iota(jnp.int32, (rows, 128), 1)
+    eye_in = eye_row == eye_lane
+    square_row = jnp.sum(jnp.where(eye_in, square_col, 0.0), axis=0, keepdims=True)
+    squares[...] = jnp.broadcast_to(square_row, squares.shape)
+    scaled = (inputs * gain_in[...].astype(f32).reshape(1, -1)).astype(bf16)
+    all_bias = jnp.concatenate(
+        [ref[...].astype(f32).reshape(1, -1) for ref in (query_bias, key_bias, value_bias)], axis=1
+    )
+    for b in range(mdl_count):
+        bias[b] = all_bias[:, b * block_width : (b + 1) * block_width]
+    pl.semaphore_wait(barrier, len(others))
+
+    sends = []
+    square_copies, block_copies = {}, {}
+    for d in far_first[:-1]:
+        square_copies[d] = send(squares, recv_squares.at[d], sq_s.at[d], sq_r.at[d], partner(0, d))
+        square_copies[d].start()
+    for d in far_first:
+        b = other(me_m, d)
+        pltpu.make_async_copy(proj_w.at[b], proj_w.at[b], block_sem.at[b]).wait()
+        part = jnp.dot(scaled, proj_w[b], preferred_element_type=f32).astype(bf16)
+        for i in range(heads_out):
+            send1[b, i] = part[:, i * HEAD_DIM : (i + 1) * HEAD_DIM]
+        if d:
+            block_copies[d] = send(send1.at[b], recv1.at[d], s1.at[d], r1.at[d], partner(0, d))
+            block_copies[d].start()
+
+    place = lax.broadcasted_iota(jnp.int32, (own_rows, HEAD_DIM), 0)
+    lane = lax.broadcasted_iota(jnp.int32, (own_rows, HEAD_DIM), 1)
+    position = place % 2
+    for r in range(local_rows):
+        position = position + jnp.where(place // 2 == r, lengths_ref[me_h * local_rows + r], 0)
+    half = HEAD_DIM // 2
+    angles = position.astype(f32) * freq_in[...]
+    cosine = jnp.cos(angles)
+    sine = jnp.sin(angles)
+    sine = jnp.where(lane < half, -sine, sine)
+
+    square_total = squares[...]
+    for d, copy in square_copies.items():
+        copy.wait()
+        square_total = square_total + recv_squares[d]
+    square_sum = jnp.sum(jnp.where(eye_in, square_total[:1, :], 0.0), axis=1, keepdims=True)
+    inv_rms = lax.rsqrt(square_sum / D + epsilon)
+    my_bias = bias[me_m]
+    for copy in block_copies.values():
+        copy.wait()
+    for i in range(heads_out):
+        total = send1[me_m, i].astype(f32)
+        for d in block_copies:
+            total = total + recv1[d, i].astype(f32)
+        total = total * inv_rms + my_bias[:, i * HEAD_DIM : (i + 1) * HEAD_DIM]
+        for h in range(hid_count):
+            send2[h, i] = total[h * own_rows : (h + 1) * own_rows].astype(bf16)
+    row_copies = {}
+    for dh, dm in others:
+        k = dh * mdl_count + dm
+        row_copies[dh, dm] = send(
+            send2.at[other(me_h, dh)], recv2.at[me_h, me_m], s2.at[k], r2.at[k], partner(dh, dm)
+        )
+        row_copies[dh, dm].start()
+    sends += row_copies.values()
+    recv2[me_h, me_m] = send2[me_h]
+
+    score_scale = 1.0 / math.sqrt(HEAD_DIM)
+    columns = lax.broadcasted_iota(jnp.int32, (pair_rows, local_len), 1)
+    pair_row = lax.broadcasted_iota(jnp.int32, (pair_rows, 128), 0)
+    pair_lane = lax.broadcasted_iota(jnp.int32, (pair_rows, 128), 1)
+    top_place = pair_row == pair_lane
+    sum_place = pair_row + pair_rows == pair_lane
+    part_copies, stat_copies, head_copies = {}, {}, {}
+
+    def prepare(dh):
+        h = other(me_h, dh)
+        for dm in far_first:
+            if dh or dm:
+                row_copies[dh, dm].wait_recv()
+        x = recv2[h].astype(f32).reshape(mdl_count * heads_out, own_rows, HEAD_DIM)
+        turned_heads = query_heads + kv_local
+        turn = x[:turned_heads]
+        swapped = pltpu.roll(turn.reshape(turned_heads * own_rows, HEAD_DIM), half, 1)
+        turned = turn * cosine[None] + swapped.reshape(turned_heads, own_rows, HEAD_DIM) * sine[None]
+        n = query_heads * own_rows
+        rotated[dh * n : (dh + 1) * n] = turned[:query_heads].reshape(n, HEAD_DIM)
+        k = kv_local * own_rows
+        key_rot[dh * k : (dh + 1) * k] = turned[query_heads:].astype(bf16).astype(f32).reshape(k, HEAD_DIM)
+        value_rot[dh * k : (dh + 1) * k] = x[turned_heads:].reshape(k, HEAD_DIM)
+        for r in range(local_rows):
+            steps = [rotated[pl.ds(dh * n + 2 * r + t, query_heads, stride=own_rows), :] for t in range(2)]
+            for kv in range(kv_local):
+                row_queries[r, dh * kv_local + kv] = jnp.concatenate(
+                    [step[kv * group : (kv + 1) * group] for step in steps], axis=0
+                ).astype(bf16)
+
+    def attend(dh):
+        wide = pl.ds(pl.multiple_of(other(me_h, dh) * 2 * HEAD_DIM, 2 * HEAD_DIM), 2 * HEAD_DIM)
+        for d in far_first:
+            r = other(me_m, d)
+            visible = columns < lengths_ref[me_h * local_rows + r] - me_m * local_len
+            qa, qb = row_queries[r, 2 * dh], row_queries[r, 2 * dh + 1]
+            none = jnp.zeros_like(qa)
+            left = jnp.concatenate(
+                [jnp.concatenate([qa, none], axis=1), jnp.concatenate([none, qb], axis=1)], axis=0
+            )
+            scores = lax.dot_general(
+                left, keys[r, :, wide], (((1,), (1,)), ((), ())), preferred_element_type=f32
+            ) * score_scale
+            masked = jnp.where(visible, scores, -1e30)
+            top = jnp.max(masked, axis=-1, keepdims=True)
+            weights = jnp.where(visible, jnp.exp(masked - top), 0.0)
+            total = jnp.sum(weights, axis=-1, keepdims=True)
+            acc = jnp.dot(weights.astype(bf16), values[r, :, wide], preferred_element_type=f32)
+            send3[dh, d, 0] = acc[:block_rows, :HEAD_DIM].astype(bf16)
+            send3[dh, d, 1] = acc[block_rows:, HEAD_DIM:].astype(bf16)
+            packed = jnp.where(top_place, top, 0.0) + jnp.where(sum_place, total, 0.0)
+            stats[dh, d] = jnp.broadcast_to(jnp.sum(packed, axis=0, keepdims=True), (8, 128))
+            if d:
+                k = dh * mdl_count + d
+                to = partner(0, d)
+                part_copies[dh, d] = send(send3.at[dh, d], recv3.at[dh, d], s3.at[k], r3.at[k], to)
+                stat_copies[dh, d] = send(stats.at[dh, d], recv_stats.at[dh, d], st_s.at[k], st_r.at[k], to)
+                part_copies[dh, d].start()
+                stat_copies[dh, d].start()
+                sends.append(part_copies[dh, d])
+                sends.append(stat_copies[dh, d])
+
+    second = lax.broadcasted_iota(jnp.int32, (pair_rows, 1), 0) % block_rows >= group
+
+    def new_part(ref, dh, t):
+        both = ref[pl.ds(dh * kv_local * own_rows + 2 * me_m + t, kv_local, stride=own_rows), :]
+        return jnp.concatenate(
+            [jnp.broadcast_to(both[kv : kv + 1], (block_rows, HEAD_DIM)) for kv in range(kv_local)], axis=0
+        )
+
+    def combine(dh):
+        query = jnp.concatenate([row_queries[me_m, 2 * dh], row_queries[me_m, 2 * dh + 1]], axis=0).astype(f32)
+        first_score = jnp.sum(query * new_part(key_rot, dh, 0), axis=-1, keepdims=True) * score_scale
+        next_score = jnp.sum(query * new_part(key_rot, dh, 1), axis=-1, keepdims=True) * score_scale
+        next_score = jnp.where(second, next_score, -1e30)
+        top = jnp.maximum(first_score, next_score)
+        for d in far_first[:-1]:
+            stat_copies[dh, d].wait_recv()
+            part_copies[dh, d].wait_recv()
+        held = [stats[dh, 0] if d == 0 else recv_stats[dh, d] for d in far_first]
+        tops = [jnp.sum(jnp.where(top_place, x[:1], 0.0), axis=1, keepdims=True) for x in held]
+        sums = [jnp.sum(jnp.where(sum_place, x[:1], 0.0), axis=1, keepdims=True) for x in held]
+        for part_top in tops:
+            top = jnp.maximum(top, part_top)
+        first_weight = jnp.exp(first_score - top)
+        next_weight = jnp.where(second, jnp.exp(next_score - top), 0.0)
+        total = first_weight + next_weight
+        mixed = first_weight.astype(bf16).astype(f32) * new_part(value_rot, dh, 0)
+        mixed = mixed + next_weight.astype(bf16).astype(f32) * new_part(value_rot, dh, 1)
+        for n, d in enumerate(far_first):
+            factor = jnp.exp(tops[n] - top)
+            acc = send3[dh, 0] if d == 0 else recv3[dh, d]
+            total = total + sums[n] * factor
+            mixed = mixed + acc.reshape(pair_rows, HEAD_DIM).astype(f32) * factor
+        send4[dh] = (mixed / total).astype(bf16)
+        for dm in far_first:
+            if dh or dm:
+                k = dh * mdl_count + dm
+                head_copies[dh, dm] = send(
+                    send4.at[dh], recv4.at[me_h, me_m], s4.at[k], r4.at[k], partner(dh, dm)
+                )
+                head_copies[dh, dm].start()
+                sends.append(head_copies[dh, dm])
+            else:
+                recv4[me_h, me_m] = send4[0]
+
+    prepare(0)
+    keys_load.wait()
+    values_load.wait()
+    for dh in range(hid_count):
+        attend(dh)
+        if dh + 1 < hid_count:
+            prepare(dh + 1)
+        if dh:
+            combine(dh - 1)
+    combine(hid_count - 1)
+
+    for copy in head_copies.values():
+        copy.wait_recv()
+    heads_f32[...] = recv4[...].astype(f32).reshape(heads_f32.shape)
+    senders = hid_count * mdl_count
+    for j in range(query_heads):
+        kv, g = j // group, j % group
+        both = [
+            heads_f32[pl.ds(kv * block_rows + t * group + g, senders, stride=pair_rows), :] for t in range(2)
+        ]
+        heads_in[:, j * HEAD_DIM : (j + 1) * HEAD_DIM] = jnp.concatenate(both, axis=0).astype(bf16)
+    out_load.wait()
+    chunks, chunk_width = send5.shape[1], send5.shape[3]
+    out_copies = {}
+    for c in range(chunks):
+        part = jnp.dot(
+            heads_in[...], out_w[:, c * chunk_width : (c + 1) * chunk_width], preferred_element_type=f32
+        )
+        for h in range(hid_count):
+            low = h * mdl_count
+            send5[h, c] = jnp.concatenate(
+                [part[low : low + mdl_count], part[senders + low : senders + low + mdl_count]], axis=0
+            ).astype(bf16)
+        for d in far_first[:-1]:
+            k = d * chunks + c
+            out_copies[d, c] = send(
+                send5.at[other(me_h, d), c], recv5.at[d, c], s5.at[k], r5.at[k], partner(d, 0)
+            )
+            out_copies[d, c].start()
+    sends += out_copies.values()
+    for c in range(chunks):
+        summed = send5[me_h, c].astype(f32)
+        for d in far_first[:-1]:
+            out_copies[d, c].wait_recv()
+            summed = summed + recv5[d, c].astype(f32)
+        result_ref[:, c * chunk_width : (c + 1) * chunk_width] = summed.astype(bf16)
+    for copy in sends:
+        copy.wait_send()
+
+
+def fused_body(
+    tokens,
+    norm_gain,
+    query_weight,
+    key_weight,
+    value_weight,
+    query_bias,
+    key_bias,
+    value_bias,
+    out_weight,
+    key_cache,
+    value_cache,
+    lengths,
+):
+    row_count, steps_count, width = tokens.shape
+    hid_count, mdl_count = lax.axis_size("hid"), lax.axis_size("mdl")
+    local_rows, local_len = key_cache.shape[:2]
+    rows = row_count * steps_count
+    own_rows = rows // hid_count
+    proj_width = query_weight.shape[1] + 2 * key_weight.shape[1]
+    block_width = proj_width // mdl_count
+    heads_out = block_width // HEAD_DIM
+    group = HEADS // KV_HEADS
+    block_rows = steps_count * group
+    kv_local = KV_HEADS // hid_count
+    out_width = out_weight.shape[1]
+    pairs = hid_count * mdl_count
+    chunks = 2
+    half = HEAD_DIM // 2
+    freq = jnp.asarray((rope_base ** (-2.0 * (np.arange(HEAD_DIM) % half) / HEAD_DIM)).astype(np.float32)[None])
+    bf16, f32 = jnp.bfloat16, jnp.float32
+    vmem, hbm = pl.BlockSpec(memory_space=pltpu.VMEM), pl.BlockSpec(memory_space=pl.ANY)
+    dma = pltpu.SemaphoreType.DMA
+    result = pl.pallas_call(
+        fused_kernel,
+        out_shape=jax.ShapeDtypeStruct((own_rows, out_width), bf16),
+        in_specs=[hbm] * 6 + [pl.BlockSpec(memory_space=pltpu.SMEM)] + [hbm] * 6,
+        out_specs=vmem,
+        scratch_shapes=[
+            pltpu.VMEM(tokens.shape, bf16),
+            pltpu.VMEM(norm_gain.shape, bf16),
+            pltpu.VMEM(query_bias.shape, bf16),
+            pltpu.VMEM(key_bias.shape, bf16),
+            pltpu.VMEM(value_bias.shape, bf16),
+            pltpu.VMEM((1, HEAD_DIM), f32),
+            pltpu.VMEM((mdl_count, 1, block_width), f32),
+            pltpu.VMEM((mdl_count, width, block_width), bf16),
+            pltpu.VMEM(out_weight.shape, bf16),
+            pltpu.VMEM(key_cache.shape, bf16),
+            pltpu.VMEM(value_cache.shape, bf16),
+            pltpu.VMEM((mdl_count, heads_out, rows, HEAD_DIM), bf16),
+            pltpu.VMEM((mdl_count, heads_out, rows, HEAD_DIM), bf16),
+            pltpu.VMEM((8, 128), f32),
+            pltpu.VMEM((mdl_count, 8, 128), f32),
+            pltpu.VMEM((hid_count, heads_out, own_rows, HEAD_DIM), bf16),
+            pltpu.VMEM((hid_count, mdl_count, heads_out, own_rows, HEAD_DIM), bf16),
+            pltpu.VMEM((HEADS * own_rows, HEAD_DIM), f32),
+            pltpu.VMEM((KV_HEADS * own_rows, HEAD_DIM), f32),
+            pltpu.VMEM((KV_HEADS * own_rows, HEAD_DIM), f32),
+            pltpu.VMEM((local_rows, KV_HEADS, block_rows, HEAD_DIM), bf16),
+            pltpu.VMEM((hid_count, mdl_count, kv_local, block_rows, HEAD_DIM), bf16),
+            pltpu.VMEM((hid_count, mdl_count, kv_local, block_rows, HEAD_DIM), bf16),
+            pltpu.VMEM((hid_count, mdl_count, 8, 128), f32),
+            pltpu.VMEM((hid_count, mdl_count, 8, 128), f32),
+            pltpu.VMEM((hid_count, kv_local * block_rows, HEAD_DIM), bf16),
+            pltpu.VMEM((hid_count, mdl_count, kv_local * block_rows, HEAD_DIM), bf16),
+            pltpu.VMEM((pairs * kv_local * block_rows, HEAD_DIM), f32),
+            pltpu.VMEM((rows, out_weight.shape[0]), bf16),
+            pltpu.VMEM((hid_count, chunks, own_rows, out_width // chunks), bf16),
+            pltpu.VMEM((hid_count, chunks, own_rows, out_width // chunks), bf16),
+            dma((9,)), dma((mdl_count,)),
+            dma((mdl_count,)), dma((mdl_count,)),
+            dma((mdl_count,)), dma((mdl_count,)),
+            dma((pairs,)), dma((pairs,)),
+            dma((pairs,)), dma((pairs,)),
+            dma((pairs,)), dma((pairs,)),
+            dma((pairs,)), dma((pairs,)),
+            dma((hid_count * chunks,)), dma((hid_count * chunks,)),
+        ],
+        compiler_params=pltpu.CompilerParams(
+            collective_id=0, has_side_effects=True, vmem_limit_bytes=60 * 2**20
+        ),
+    )(
+        tokens, norm_gain, query_bias, key_bias, value_bias, freq, lengths,
+        query_weight, key_weight, value_weight, out_weight, key_cache, value_cache,
+    )
+    return result.reshape(steps_count, local_rows, out_width).transpose(1, 0, 2)
+
+
+def choose(*arrays):
+    tokens, query_weight, key_weight, key_cache = arrays[0], arrays[2], arrays[3], arrays[9]
+    hid_count, mdl_count = lax.axis_size("hid"), lax.axis_size("mdl")
+    proj_width = query_weight.shape[1] + 2 * key_weight.shape[1]
+    fits = (
+        tokens.shape[1] == 2
+        and mdl_count == 4
+        and key_cache.shape[0] == mdl_count
+        and key_weight.shape[1] == 2 * HEAD_DIM
+        and KV_HEADS == 2 * hid_count
+        and proj_width % (mdl_count * HEAD_DIM) == 0
+        and (mdl_count - 1) * proj_width <= mdl_count * query_weight.shape[1]
+        and tokens.shape[0] * 2 <= 128
+    )
+    return (fused_body if fits else body)(*arrays)
+
 
 def solution(mesh):
     placed = (
@@ -187,7 +602,7 @@
         P("groups"),
     )
     return jax.shard_map(
-        body,
+        choose,
         mesh=mesh,
         in_specs=placed,
         out_specs=P(("groups", "hid"), None, "mdl"),

time: 193 us -> 41.4 us (0.21)
  blocking collectives: 61.8 us -> 0 us
  waiting for transfers between devices: 46.7 us -> 0 us
  Pallas kernels: 0 us -> 39.8 us
  local copies, waits for them, and re-layouts: 36 us -> 1.43 us
  matrix products: 24.2 us -> 0 us
  between operations: 13.7 us -> 0.01 us
  other arithmetic: 5.87 us -> 0 us
  starting transfers between devices: 3.39 us -> 0 us
    all_gather x3 -> x0, blocking collectives: 41.1 us -> none  [combined_all(): lax.all_gather(part.astype(kind), axis)]
    pallas_call x0 -> x1, Pallas kernels: none -> 39.8 us  [fused_body(): pl.pallas_call(fused_kernel, out_shape=jax.ShapeDtypeStruct((own_rows, ou...]
    dot_general x8 -> x0, matrix products: 24.2 us -> none  [the longest x1 5.78 us: body(): jnp.einsum('rkqd,rskd->rkqs', grouped, cache_keys, preferred_element_type...]
    psum x1 -> x0, waiting for transfers between devices: 23.2 us -> none  [body(): lax.psum(partial_value.astype(jnp.bfloat16), 'mdl').astype(jnp.float32)]
    unnamed x12 -> x0, local copies, waits for them, and re-layouts: 18.7 us -> none
    reduce_scatter x1 -> x0, waiting for transfers between devices: 18.6 us -> none  [body(): lax.psum_scatter(jnp.dot(flat_heads, out_weight, preferred_element_type=j...]
    psum x1 -> x0, blocking collectives: 13.7 us -> none  [body(): square_sum = lax.psum(jnp.sum(inputs * inputs, axis=-1), 'mdl')]
    all_to_all x2 -> x0, local copies, waits for them, and re-layouts: 9.78 us -> none  [the longest x1 9.69 us: body(): lax.all_to_all(attended, 'hid', split_axis=2, concat_axis=0, tiled=True)]
  transfers between devices with their start and end apart: 3 -> 0, of which waited for: 3 -> 0; matrix products, arithmetic and copies ran while one was open for 0% -> 0% of each run, Pallas kernels for 0% -> 0%
where the time goes in v2:
time: 41.4 us; the launch traced here: 41.2 us
  Pallas kernels  39.8 us (96%)
  local copies, waits for them, and re-layouts  1.43 us (3%)
    pallas_call x1, Pallas kernels, fused_body(): pl.pallas_call(fused_kernel, out_shape=jax.ShapeDtypeStruct((own_rows, ou...  39.8 us
    reshape x2, local copies, waits for them, and re-layouts, fused_body(): return result.reshape(steps_count, local_rows, out_width).transpose(1, 0, 2)  1.43 us

profile of v2, /device:TPU:0, one launch (start us, length us, event | category | flops | bytes accessed | tf_op | source)
XLA Modules:
  0.0 41.2 jit_solution(5231204818951352750)
XLA Ops:
  0.0 39.8 %shard_map.127 = bf16[8,2048]{1,0:T(8,128)(2,1)} custom-call(bf16[16,2,2048]{2,1,0:T(2,128)(2,1)} %tokens_hbm.1, bf16[2048]{0:T(1024)(128)(2,1)} %gain_hbm.1, bf16[2048]{0:T(1024)(128)(2,1)} %query_bias_hbm.1, bf16[256]{0:T(256)(128)(2,1)} %key_bias_hbm.1, bf16[256]{0:T(256)(128)(2,1)} %value_bias_hbm.1, f32[1,128]{1,0:T(1,128)} %constant.2.clone.freq_hbm, ...), custom_call_target="tpu_custom_call" | custom-call | tf_op jit(solution)/shard_map/pallas_call | solution.py:516
  39.8 0.8 %reshape.3 = bf16[2,4,2048]{2,1,0:T(4,128)(2,1)S(1)} reshape(bf16[8,2048]{1,0:T(8,128)(2,1)} %shard_map.127) | data formatting | bytes 65536 | tf_op jit(solution)/shard_map/reshape | solution.py:569
  40.5 0.6 %copy.16 = bf16[2,4,2048]{2,0,1:T(2,128)(2,1)} copy(bf16[2,4,2048]{2,1,0:T(4,128)(2,1)S(1)} %reshape.3) | data formatting | bytes 65536 | tf_op jit(solution)/shard_map/reshape | solution.py:569
